TPU v7x, 32 devices: a whole 2x2x4 slice. The times are simulated.
32 devices in a mesh: ctx: 8 (over z, y), fsdp: 4 (over x, core).
Axes of the slice: x: 2, y: 2, z: 4, core: 2. Of those that a mesh axis runs over, the one named last changes fastest.
Arguments:
- tokens: bfloat16 [4, 16, 128, 1024], P('fsdp', None, 'ctx'), may hold values from -6 to 6
- lengths: int32 [4, 3], P('fsdp'), may hold values from 512 to 1024, as said below
- packing: int32 [4, 3], P('fsdp'), may hold values from 0 to 2, each once within a row
- query_w: bfloat16 [1024, 1024], P('fsdp'), may hold values from -0.1875 to 0.1875
- query_b: float32 [1024], replicated, may hold values from -3 to 3
- key_w: bfloat16 [1024, 1024], P('fsdp'), may hold values from -0.1875 to 0.1875
- value_w: bfloat16 [1024, 1024], P('fsdp'), may hold values from -0.1875 to 0.1875
- value_b: float32 [1024], replicated, may hold values from -3 to 3
- output_w: bfloat16 [1024, 1024], P('fsdp'), may hold values from -3 to 3
- output_b: float32 [1024], replicated, may hold values from -3 to 3
- attn_gain: float32 [1024], replicated, may hold values from 0.5 to 1.5
- attn_shift: float32 [1024], replicated, may hold values from -2 to 2
- expand_w: bfloat16 [1024, 4096], P('fsdp'), may hold values from -0.1875 to 0.1875
- expand_b: float32 [4096], replicated, may hold values from -3 to 3
- reduce_w: bfloat16 [4096, 1024], P('fsdp'), may hold values from -0.09375 to 0.09375
- reduce_b: float32 [1024], replicated, may hold values from -3 to 3
- ffn_gain: float32 [1024], replicated, may hold values from 0.5 to 1.5
- ffn_shift: float32 [1024], replicated, may hold values from -2 to 2
- cotangent: bfloat16 [4, 16, 128, 1024], P('fsdp', None, 'ctx'), may hold values from -6 to 6
Outputs:
- layer_out: bfloat16 [4, 16, 128, 1024], P('fsdp', None, 'ctx')
- grad_tokens: float32 [4, 16, 128, 1024], P('fsdp', None, 'ctx')
- grad_query_w: float32 [1024, 1024], P('fsdp')
- grad_query_b: float32 [1024], replicated
- grad_key_w: float32 [1024, 1024], P('fsdp')
- grad_value_w: float32 [1024, 1024], P('fsdp')
- grad_value_b: float32 [1024], replicated
- grad_output_w: float32 [1024, 1024], P('fsdp')
- grad_output_b: float32 [1024], replicated
- grad_attn_gain: float32 [1024], replicated
- grad_attn_shift: float32 [1024], replicated
- grad_expand_w: float32 [1024, 4096], P('fsdp')
- grad_expand_b: float32 [4096], replicated
- grad_reduce_w: float32 [4096, 1024], P('fsdp')
- grad_reduce_b: float32 [1024], replicated
- grad_ffn_gain: float32 [1024], replicated
- grad_ffn_shift: float32 [1024], replicated
Inputs may be any that keep to these rules, and one draw needn't show every extreme that they name: Each row's 3 lengths sum to 2048. Each row of packing names every sequence once.
All inputs are finite; a program needn't handle non-finite values.
Results may differ from a plain program's by a relative error of at most 0.02.
Values may be sent and summed in bfloat16 or wider, within the bound.
A program may use at most 192 MiB of HBM per device.

v0:
```python
import jax
import jax.numpy as jnp
from jax import lax
from jax.sharding import PartitionSpec as P

H = 16
HD = 64


def from_behind(block, axis, distance):
    devices = range(lax.axis_size(axis))
    route = [((i - distance) % len(devices), i) for i in devices]
    return lax.ppermute(block, axis, route)


def dense(left, right):
    return jnp.dot(left, right, preferred_element_type=jnp.float32)


def dense_back(left, right):
    return lax.dot_general(
        left, right, (((1,), (1,)), ((), ())), preferred_element_type=jnp.float32
    )


def norm_fwd(hidden, gain, shift):
    mean_row = jnp.mean(hidden, axis=-1, keepdims=True)
    centred = hidden - mean_row
    variance = jnp.mean(centred * centred, axis=-1, keepdims=True)
    inv_std = lax.rsqrt(variance + 1e-05)
    x_hat = centred * inv_std
    return (x_hat * gain + shift, x_hat, inv_std)


def norm_back(incoming, x_hat, inv_std, gain):
    scaled = incoming * gain
    grad_in = inv_std * (
        scaled
        - jnp.mean(scaled, axis=-1, keepdims=True)
        - x_hat * jnp.mean(scaled * x_hat, axis=-1, keepdims=True)
    )
    return (grad_in, jnp.sum(incoming * x_hat, axis=0), jnp.sum(incoming, axis=0))


def gelu_slope(pre_act):
    return (
        0.5 * (1.0 + lax.erf(pre_act * 0.7071067811865476))
        + pre_act * jnp.exp(-0.5 * pre_act * pre_act) * 0.3989422804014327
    )


def online_update(running, query_heads, query_seg, key_rows, value_rows, key_seg):
    accum, run_max, run_sum = running
    rows_here = key_rows.shape[0]
    scores = 0.125 * jnp.einsum(
        "qhd,khd->hqk",
        query_heads,
        key_rows.reshape(rows_here, H, HD),
        preferred_element_type=jnp.float32,
    )
    same_seg = (query_seg[:, None] == key_seg[None, :])[None]
    masked = jnp.where(same_seg, scores, -1e30)
    new_max = jnp.maximum(run_max, jnp.max(masked, axis=-1))
    scale_old = jnp.exp(run_max - new_max)
    exp_scores = jnp.where(same_seg, jnp.exp(masked - new_max[:, :, None]), 0.0)
    run_sum = run_sum * scale_old + jnp.sum(exp_scores, axis=-1)
    update = jnp.einsum(
        "hqk,khd->qhd",
        exp_scores.astype(jnp.bfloat16),
        value_rows.reshape(rows_here, H, HD),
        preferred_element_type=jnp.float32,
    )
    accum = accum * scale_old.T[:, :, None] + update
    return (accum, new_max, run_sum)


def pair_grads(query_rows, grad_rows, log_sum, delta_row, query_seg, key_rows, value_rows, key_seg):
    q_heads = query_rows.reshape(-1, H, HD)
    g_heads = grad_rows.reshape(-1, H, HD)
    k_heads = key_rows.reshape(-1, H, HD)
    v_heads = value_rows.reshape(-1, H, HD)
    scores = 0.125 * jnp.einsum(
        "qhd,khd->hqk", q_heads, k_heads, preferred_element_type=jnp.float32
    )
    same_seg = (query_seg[:, None] == key_seg[None, :])[None]
    probs = jnp.where(
        same_seg, jnp.exp(jnp.where(same_seg, scores, -1e30) - log_sum[:, :, None]), 0.0
    )
    grad_prob = jnp.einsum("qhd,khd->hqk", g_heads, v_heads, preferred_element_type=jnp.float32)
    grad_score = (probs * (grad_prob - delta_row[:, :, None])).astype(jnp.bfloat16)
    grad_q = 0.125 * jnp.einsum(
        "hqk,khd->qhd", grad_score, k_heads, preferred_element_type=jnp.float32
    )
    grad_k = 0.125 * jnp.einsum(
        "hqk,qhd->khd", grad_score, q_heads, preferred_element_type=jnp.float32
    )
    grad_v = jnp.einsum(
        "hqk,qhd->khd", probs.astype(jnp.bfloat16), g_heads, preferred_element_type=jnp.float32
    )
    return (
        grad_q.reshape(query_rows.shape),
        grad_k.reshape(key_rows.shape),
        grad_v.reshape(key_rows.shape),
    )


def owner_rows(layer_in, layer_grad):
    return lax.psum_scatter(
        lax.dot_general(
            layer_in, layer_grad, (((0,), (0,)), ((), ())), preferred_element_type=jnp.float32
        ).astype(jnp.bfloat16),
        "fsdp",
        scatter_dimension=0,
        tiled=True,
    ).astype(jnp.float32)


def body(
    tokens,
    lengths,
    packing,
    query_w,
    query_b,
    key_w,
    value_w,
    value_b,
    output_w,
    output_b,
    attn_gain,
    attn_shift,
    expand_w,
    expand_b,
    reduce_w,
    reduce_b,
    ffn_gain,
    ffn_shift,
    cotangent,
):
    tok_shape = tokens.shape
    stripe = tok_shape[2]
    block_len = tok_shape[1] * tok_shape[2]
    model_width = tok_shape[3]
    n_ctx = lax.axis_size("ctx")
    ctx_index = lax.axis_index("ctx")
    seq_lens = lengths[0]
    slot_ids = packing[0]
    ordered = jnp.sum(
        jnp.where(
            slot_ids[:, None] == jnp.arange(seq_lens.shape[0], dtype=jnp.int32)[None, :],
            seq_lens[None, :],
            0,
        ),
        axis=1,
    )
    slot_ends = jnp.cumsum(ordered)
    gathered = jnp.arange(n_ctx * block_len, dtype=jnp.int32)
    owner_dev = gathered // block_len
    local_row = gathered % block_len
    position = local_row // stripe * (stripe * n_ctx) + owner_dev * stripe + local_row % stripe
    seg_all = jnp.sum((position[:, None] >= slot_ends[None, :]).astype(jnp.int32), axis=1)
    query_seg = lax.dynamic_slice_in_dim(seg_all, ctx_index * block_len, block_len)
    inputs = tokens.reshape(block_len, model_width)
    w_query, w_key, w_value, w_output, w_up, w_down = (
        lax.all_gather(query_w, "fsdp", axis=0, tiled=True),
        lax.all_gather(key_w, "fsdp", axis=0, tiled=True),
        lax.all_gather(value_w, "fsdp", axis=0, tiled=True),
        lax.all_gather(output_w, "fsdp", axis=0, tiled=True),
        lax.all_gather(expand_w, "fsdp", axis=0, tiled=True),
        lax.all_gather(reduce_w, "fsdp", axis=0, tiled=True),
    )
    queries = (dense(inputs, w_query) + query_b).astype(jnp.bfloat16)
    key_rows = dense(inputs, w_key).astype(jnp.bfloat16)
    values = (dense(inputs, w_value) + value_b).astype(jnp.bfloat16)
    query_heads = queries.reshape(block_len, H, HD)
    start_state = (
        jnp.zeros((block_len, H, HD), jnp.float32),
        jnp.full((H, block_len), -1e30, jnp.float32),
        jnp.zeros((H, block_len), jnp.float32),
    )
    key_piece = lax.all_gather(key_rows, "ctx", axis=0, tiled=True)
    value_piece = lax.all_gather(values, "ctx", axis=0, tiled=True)
    shards = key_piece.shape[0] // block_len

    def one_shard(index, inner):
        key_part = lax.dynamic_slice_in_dim(key_piece, index * block_len, block_len)
        value_part = lax.dynamic_slice_in_dim(value_piece, index * block_len, block_len)
        key_seg = lax.dynamic_slice_in_dim(seg_all, index * block_len, block_len)
        return online_update(inner, query_heads, query_seg, key_part, value_part, key_seg)

    accum, run_max, run_sum = lax.fori_loop(0, shards, one_shard, start_state)
    attended = (accum / run_sum.T[:, :, None]).reshape(block_len, model_width).astype(jnp.bfloat16)
    log_sum = run_max + jnp.log(run_sum)
    branch = dense(attended, w_output) + output_b
    normed, x_hat1, inv_std1 = norm_fwd(inputs.astype(jnp.float32) + branch, attn_gain, attn_shift)
    normed_low = normed.astype(jnp.bfloat16)
    pre_act = dense(normed_low, w_up) + expand_b
    hidden = jax.nn.gelu(pre_act, approximate=False).astype(jnp.bfloat16)
    ffn_out = dense(hidden, w_down) + reduce_b
    outputs, x_hat2, inv_std2 = norm_fwd(normed + ffn_out, ffn_gain, ffn_shift)
    layer_out = outputs.astype(jnp.bfloat16).reshape(tok_shape)
    upstream = cotangent.reshape(block_len, model_width).astype(jnp.float32)
    grad_mid2, grad_ffn_gain, grad_ffn_shift = norm_back(upstream, x_hat2, inv_std2, ffn_gain)
    grad_ffn = grad_mid2.astype(jnp.bfloat16)
    grad_reduce_b = jnp.sum(grad_ffn.astype(jnp.float32), axis=0)
    share_down = owner_rows(hidden, grad_ffn)
    grad_pre = (dense_back(grad_ffn, w_down) * gelu_slope(pre_act)).astype(jnp.bfloat16)
    grad_expand_b = jnp.sum(grad_pre.astype(jnp.float32), axis=0)
    share_up = owner_rows(normed_low, grad_pre)
    grad_normed = dense_back(grad_pre, w_up) + grad_mid2
    grad_mid1, grad_attn_gain, grad_attn_shift = norm_back(grad_normed, x_hat1, inv_std1, attn_gain)
    grad_branch = grad_mid1.astype(jnp.bfloat16)
    grad_output_b = jnp.sum(grad_branch.astype(jnp.float32), axis=0)
    share_out = owner_rows(attended, grad_branch)
    grad_att = dense_back(grad_branch, w_output).astype(jnp.bfloat16)
    delta_row = jnp.einsum(
        "qhd,qhd->hq",
        grad_att.astype(jnp.float32).reshape(block_len, H, HD),
        attended.astype(jnp.float32).reshape(block_len, H, HD),
    )
    zero_rows = jnp.zeros((block_len, model_width), jnp.float32)

    def key_step(step, state):
        visit_keys, visit_values, sum_k, sum_v, sum_q = state
        anchor = (ctx_index - step) % n_ctx
        key_seg = lax.dynamic_slice_in_dim(seg_all, anchor * block_len, block_len)
        part_q, part_k, part_v = pair_grads(
            queries, grad_att, log_sum, delta_row, query_seg, visit_keys, visit_values, key_seg
        )
        sum_q = sum_q + part_q
        visit_keys, visit_values = from_behind((visit_keys, visit_values), "ctx", 1)
        sum_k, sum_v = (
            from_behind((sum_k + part_k).astype(jnp.bfloat16), "ctx", 1).astype(jnp.float32),
            from_behind((sum_v + part_v).astype(jnp.bfloat16), "ctx", 1).astype(jnp.float32),
        )
        return (visit_keys, visit_values, sum_k, sum_v, sum_q)

    final = lax.fori_loop(0, n_ctx, key_step, (key_rows, values, zero_rows, zero_rows, zero_rows))
    sum_k, sum_v, sum_q = (final[2], final[3], final[4])
    grad_q = sum_q.astype(jnp.bfloat16)
    grad_k = sum_k.astype(jnp.bfloat16)
    grad_v = sum_v.astype(jnp.bfloat16)
    grad_query_b = jnp.sum(grad_q.astype(jnp.float32), axis=0)
    grad_value_b = jnp.sum(grad_v.astype(jnp.float32), axis=0)
    share_query = owner_rows(inputs, grad_q)
    share_key = owner_rows(inputs, grad_k)
    share_value = owner_rows(inputs, grad_v)
    grad_inputs = (
        dense_back(grad_q, w_query)
        + dense_back(grad_k, w_key)
        + dense_back(grad_v, w_value)
        + grad_mid1
    )
    share_query, share_key, share_value, share_out, share_up, share_down = lax.psum(
        (share_query, share_key, share_value, share_out, share_up, share_down), "ctx"
    )
    (
        grad_query_b,
        grad_value_b,
        grad_output_b,
        grad_attn_gain,
        grad_attn_shift,
        grad_expand_b,
        grad_reduce_b,
        grad_ffn_gain,
        grad_ffn_shift,
    ) = lax.psum(
        (
            grad_query_b,
            grad_value_b,
            grad_output_b,
            grad_attn_gain,
            grad_attn_shift,
            grad_expand_b,
            grad_reduce_b,
            grad_ffn_gain,
            grad_ffn_shift,
        ),
        ("ctx", "fsdp"),
    )
    return (
        layer_out,
        grad_inputs.reshape(tok_shape),
        share_query,
        grad_query_b,
        share_key,
        share_value,
        grad_value_b,
        share_out,
        grad_output_b,
        grad_attn_gain,
        grad_attn_shift,
        share_up,
        grad_expand_b,
        share_down,
        grad_reduce_b,
        grad_ffn_gain,
        grad_ffn_shift,
    )


def solution(mesh):
    return jax.shard_map(
        body,
        mesh=mesh,
        in_specs=(
            P("fsdp", None, "ctx", None),
            P("fsdp", None),
            P("fsdp", None),
            P("fsdp", None),
            P(),
            P("fsdp", None),
            P("fsdp", None),
            P(),
            P("fsdp", None),
            P(),
            P(),
            P(),
            P("fsdp", None),
            P(),
            P("fsdp", None),
            P(),
            P(),
            P(),
            P("fsdp", None, "ctx", None),
        ),
        out_specs=(
            P("fsdp", None, "ctx", None),
            P("fsdp", None, "ctx", None),
            P("fsdp", None),
            P(),
            P("fsdp", None),
            P("fsdp", None),
            P(),
            P("fsdp", None),
            P(),
            P(),
            P(),
            P("fsdp", None),
            P(),
            P("fsdp", None),
            P(),
            P(),
            P(),
        ),
        check_vma=False,
    )
```

profile of v0, /device:TPU:0, one launch (start us, length us, event | category | flops | bytes accessed | tf_op | source)
XLA Modules:
  0.0 1580.0 jit_solution(11764506689131481254)
XLA Ops:
  9.5 25.4 %all-gather.9.cloned.1.call-done = bf16[1024,1024]{1,0:T(8,128)(2,1)} async-done(((bf16[256,1024]{1,0:T(8,128)(2,1)}), bf16[1024,1024]{1,0:T(8,128)(2,1)}) %all-gather.9.cloned.1.call-update) | async-done | bytes 2097168 | tf_op jit(solution)/shard_map/all_gather | solution.py:165
  38.3 20.8 %all-gather.15.cloned.1.call-done = bf16[1024,1024]{1,0:T(8,128)(2,1)} async-done(((bf16[256,1024]{1,0:T(8,128)(2,1)}), bf16[1024,1024]{1,0:T(8,128)(2,1)}) %all-gather.15.cloned.1.call-update) | async-done | bytes 2097168 | tf_op jit(solution)/shard_map/all_gather | solution.py:166
  67.9 15.4 all-gather.13.cloned.1.call-done
  85.8 73.5 %all-gather.11.cloned.1.call-done = bf16[2048,1024]{1,0:T(8,128)(2,1)} async-done(((bf16[256,1024]{1,0:T(8,128)(2,1)}), bf16[2048,1024]{1,0:T(8,128)(2,1)}) %all-gather.11.cloned.1.call-update) | async-done | bytes 4194320 | tf_op jit(solution)/shard_map/all_gather | solution.py:180
  159.3 74.2 %all-gather.17.cloned.1.call-done = bf16[2048,1024]{1,0:T(8,128)(2,1)} async-done(((bf16[256,1024]{1,0:T(8,128)(2,1)}), bf16[2048,1024]{1,0:T(8,128)(2,1)}) %all-gather.17.cloned.1.call-update) | async-done | bytes 4194320 | tf_op jit(solution)/shard_map/all_gather | solution.py:181
  233.5 103.5 %while.42 = (s32[]{:T(128)}, f32[256,16,64]{0,2,1:T(8,128)}, f32[16,256]{1,0:T(8,128)S(1)}, f32[16,256]{1,0:T(8,128)S(1)}, s32[256]{0:T(256)S(1)}, /*index=5*/s3...) while((s32[]{:T(128)}, f32[256,16,64]{0,2,1:T(8,128)}, ...), condition=%wide.region_6.7_spmd.clone, body=%wide.region_3.6_spmd.clone.sunk | while | flops 282943488 | bytes 20975804 | solution.py:190
  341.4 15.8 fusion.29
  357.2 18.4 %all-gather.23.cloned.1.call-done = bf16[4096,1024]{1,0:T(8,128)(2,1)} async-done(((bf16[1024,1024]{1,0:T(8,128)(2,1)}), bf16[4096,1024]{1,0:T(8,128)(2,1)}) %all-gather.23.cloned.1.call-update) | async-done | bytes 8388624 | tf_op jit(solution)/shard_map/all_gather | solution.py:169
  393.9 406.6 %while.43 = (s32[]{:T(128)}, bf16[256,1024]{0,1:T(8,128)(2,1)}, bf16[256,1024]{0,1:T(8,128)(2,1)}, f32[256,1024]{0,1:T(8,128)}, f32[256,1024]{0,1:T(8,128)}, /*i...) while((s32[]{:T(128)}, bf16[256,1024]{0,1:T(8,128)(2,1)}, ...), condition=%wide.region_16.17_spmd.clone, body=%wide.region_15.16_spmd.clone.sunk | while | flops 686882816 | bytes 68932264 | solution.py:237
  414.0 21.3 %collective-permute-done.2 = bf16[256,1024]{0,1:T(8,128)(2,1)} collective-permute-done((bf16[256,1024]{0,1:T(8,128)(2,1)}, bf16[256,1024]{0,1:T(8,128)(2,1)}, u32[]{:S(2)}, u32[]{:S(2)}) %collective-permute-start.2) | collective-permute-done | bytes 524320 | tf_op jit(solution)/shard_map/while/body/eval_jaxpr/ppermute | solution.py:13
  437.5 8.5 collective-permute-done.3
  466.2 23.3 %collective-permute-done.2 = bf16[256,1024]{0,1:T(8,128)(2,1)} collective-permute-done((bf16[256,1024]{0,1:T(8,128)(2,1)}, bf16[256,1024]{0,1:T(8,128)(2,1)}, u32[]{:S(2)}, u32[]{:S(2)}) %collective-permute-start.2) | collective-permute-done | bytes 524320 | tf_op jit(solution)/shard_map/while/body/eval_jaxpr/ppermute | solution.py:13
  517.6 25.1 %collective-permute-done.2 = bf16[256,1024]{0,1:T(8,128)(2,1)} collective-permute-done((bf16[256,1024]{0,1:T(8,128)(2,1)}, bf16[256,1024]{0,1:T(8,128)(2,1)}, u32[]{:S(2)}, u32[]{:S(2)}) %collective-permute-start.2) | collective-permute-done | bytes 524320 | tf_op jit(solution)/shard_map/while/body/eval_jaxpr/ppermute | solution.py:13
  568.0 26.8 %collective-permute-done.2 = bf16[256,1024]{0,1:T(8,128)(2,1)} collective-permute-done((bf16[256,1024]{0,1:T(8,128)(2,1)}, bf16[256,1024]{0,1:T(8,128)(2,1)}, u32[]{:S(2)}, u32[]{:S(2)}) %collective-permute-start.2) | collective-permute-done | bytes 524320 | tf_op jit(solution)/shard_map/while/body/eval_jaxpr/ppermute | solution.py:13
  618.9 27.2 %collective-permute-done.2 = bf16[256,1024]{0,1:T(8,128)(2,1)} collective-permute-done((bf16[256,1024]{0,1:T(8,128)(2,1)}, bf16[256,1024]{0,1:T(8,128)(2,1)}, u32[]{:S(2)}, u32[]{:S(2)}) %collective-permute-start.2) | collective-permute-done | bytes 524320 | tf_op jit(solution)/shard_map/while/body/eval_jaxpr/ppermute | solution.py:13
  669.2 27.2 %collective-permute-done.2 = bf16[256,1024]{0,1:T(8,128)(2,1)} collective-permute-done((bf16[256,1024]{0,1:T(8,128)(2,1)}, bf16[256,1024]{0,1:T(8,128)(2,1)}, u32[]{:S(2)}, u32[]{:S(2)}) %collective-permute-start.2) | collective-permute-done | bytes 524320 | tf_op jit(solution)/shard_map/while/body/eval_jaxpr/ppermute | solution.py:13
  718.6 26.6 %collective-permute-done.2 = bf16[256,1024]{0,1:T(8,128)(2,1)} collective-permute-done((bf16[256,1024]{0,1:T(8,128)(2,1)}, bf16[256,1024]{0,1:T(8,128)(2,1)}, u32[]{:S(2)}, u32[]{:S(2)}) %collective-permute-start.2) | collective-permute-done | bytes 524320 | tf_op jit(solution)/shard_map/while/body/eval_jaxpr/ppermute | solution.py:13
  767.1 25.7 %collective-permute-done.2 = bf16[256,1024]{0,1:T(8,128)(2,1)} collective-permute-done((bf16[256,1024]{0,1:T(8,128)(2,1)}, bf16[256,1024]{0,1:T(8,128)(2,1)}, u32[]{:S(2)}, u32[]{:S(2)}) %collective-permute-start.2) | collective-permute-done | bytes 524320 | tf_op jit(solution)/shard_map/while/body/eval_jaxpr/ppermute | solution.py:13
  829.5 38.5 %all-reduce = (f32[1024]{0:T(1024)}, f32[1024]{0:T(1024)}, f32[1024]{0:T(1024)}, f32[1024]{0:T(1024)}, f32[1024]{0:T(1024)}, /*index=5*/f32[4096]{0:T(1024)}, f32[1024]{0:T(1024)}, f32[1024]{0:T(1024)}, f32[1024]{0:T(1024)}) all-reduce(f32[1024]{0:T(1024)S(1)} %convert_reduce_fusion.5, ...), channel_id=1, replica_groups=mesh['ctx'=8,'fsdp'=4] {'ctx','fsdp'}, use_global_device_ids=true, to_apply=%region_20.21 | all-reduce | flops 12288 | bytes 98304 | tf_op jit(solution)/shard_map/psum | solution.py:266
  874.6 26.9 %reduce-scatter.11.cloned.1.call-done = bf16[256,1024]{0,1:T(8,128)(2,1)} async-done(((bf16[1024,1024]{0,1:T(8,128)(2,1)}), bf16[256,1024]{0,1:T(8,128)(2,1)}) %reduce-scatter.11.cloned.1.call-update) | async-done | bytes 524304 | tf_op jit(solution)/shard_map/reduce_scatter | solution.py:108
  901.5 34.0 %reduce-scatter.13.cloned.1.call-done = bf16[256,1024]{1,0:T(8,128)(2,1)} async-done(((bf16[1024,1024]{1,0:T(8,128)(2,1)}), bf16[256,1024]{1,0:T(8,128)(2,1)}) %reduce-scatter.13.cloned.1.call-update) | async-done | bytes 524304 | tf_op jit(solution)/shard_map/reduce_scatter | solution.py:108
  935.5 74.3 %reduce-scatter.15.cloned.1.call-done = bf16[256,4096]{1,0:T(8,128)(2,1)} async-done(((bf16[1024,4096]{1,0:T(8,128)(2,1)}), bf16[256,4096]{1,0:T(8,128)(2,1)}) %reduce-scatter.15.cloned.1.call-update) | async-done | bytes 2097168 | tf_op jit(solution)/shard_map/reduce_scatter | solution.py:108
  1009.8 74.4 %reduce-scatter.17.cloned.1.call-done = bf16[1024,1024]{1,0:T(8,128)(2,1)} async-done(((bf16[4096,1024]{1,0:T(8,128)(2,1)}), bf16[1024,1024]{1,0:T(8,128)(2,1)}) %reduce-scatter.17.cloned.1.call-update) | async-done | bytes 2097168 | tf_op jit(solution)/shard_map/reduce_scatter | solution.py:108
  1084.2 485.1 %all-reduce.3 = (f32[256,1024]{0,1:T(8,128)S(1)}, f32[256,1024]{0,1:T(8,128)S(1)}, f32[256,1024]{0,1:T(8,128)S(1)}, f32[256,1024]{1,0:T(8,128)}, f32[256,4096]{1,0:T(8,128)}, /*index=5*/f32[1024,1024]{1,0:T(8,128)}) all-reduce(bf16[256,1024]{0,1:T(8,128)(2,1)} %reduce-scatter.7.cloned.1.call-done, ...), channel_id=1, replica_groups=mesh['ctx'=8,'fsdp'=4] {'ctx'}, use_global_device_ids=true, to_apply=%region_18.19 | all-reduce | flops 3145728 | bytes 18874368 | tf_op jit(solution)/shard_map/psum | solution.py:253
  (511 shorter events, 375.4 us)
Async XLA Ops:
  7.9 51.2 %all-gather.15.cloned.1.call-start = ((), (), s32[]{:S(2)}) async-start(), calls=%async_computation.9 | async-start | bytes 2621440 | tf_op jit(solution)/shard_map/all_gather | solution.py:166
  8.7 74.6 %all-gather.13.cloned.1.call-start = ((), (), s32[]{:S(2)}) async-start(), calls=%async_computation.8 | async-start | bytes 2621440 | tf_op jit(solution)/shard_map/all_gather | solution.py:164
  9.4 149.9 %all-gather.11.cloned.1.call-start = ((), (), s32[]{:S(2)}) async-start(), calls=%async_computation.7 | async-start | bytes 4718592 | tf_op jit(solution)/shard_map/all_gather | solution.py:180
  38.3 195.3 %all-gather.17.cloned.1.call-start = ((), (), s32[]{:S(2)}) async-start(), calls=%async_computation.10 | async-start | bytes 4718592 | tf_op jit(solution)/shard_map/all_gather | solution.py:181
  62.2 276.2 %all-gather.19.cloned.1.call-start = ((), (), s32[]{:S(2)}) async-start(), calls=%async_computation.11 | async-start | bytes 2621440 | tf_op jit(solution)/shard_map/all_gather | solution.py:167
  62.8 278.6 %all-gather.21.cloned.1.call-start = ((), (), s32[]{:S(2)}) async-start(), calls=%async_computation.12 | async-start | bytes 10485760 | tf_op jit(solution)/shard_map/all_gather | solution.py:168
  63.6 312.0 %all-gather.23.cloned.1.call-start = ((), (), s32[]{:S(2)}) async-start(), calls=%async_computation.13 | async-start | bytes 10485760 | tf_op jit(solution)/shard_map/all_gather | solution.py:169
  64.3 810.3 %reduce-scatter.7.cloned.1.call-start = ((), (), s32[]{:S(2)}) async-start(), calls=%async_computation.14 | async-start | bytes 2621440 | tf_op jit(solution)/shard_map/reduce_scatter | solution.py:108
  395.4 52.7 %collective-permute-start = (bf16[256,1024]{0,1:T(8,128)(2,1)S(1)}, bf16[256,1024]{0,1:T(8,128)(2,1)}, u32[]{:S(2)}, u32[]{:S(2)}) collective-permute-start(bf16[256,1024]{0,1:T(8,128)(2,1)S(1)} %copy.106), channel_id=1, source_target_pairs={{28,0},{0,4},{4,8},{8,12},{12,16},{16,20},{20,24},{24,28},{29,1},{... | collective-permute-start | bytes 1572872 | tf_op jit(solution)/shard_map/while/body/eval_jaxpr/ppermute | solution.py:13
  398.7 49.3 %collective-permute-start.1 = (bf16[256,1024]{0,1:T(8,128)(2,1)}, bf16[256,1024]{0,1:T(8,128)(2,1)}, u32[]{:S(2)}, u32[]{:S(2)}) collective-permute-start(bf16[256,1024]{0,1:T(8,128)(2,1)} %copy.107), channel_id=1, source_target_pairs={{28,0},{0,4},{4,8},{8,12},{12,16},{16,20},{20,24},{24,28},{29,1},{... | collective-permute-start | bytes 1572872 | tf_op jit(solution)/shard_map/while/body/eval_jaxpr/ppermute | solution.py:13
  449.3 51.9 %collective-permute-start = (bf16[256,1024]{0,1:T(8,128)(2,1)S(1)}, bf16[256,1024]{0,1:T(8,128)(2,1)}, u32[]{:S(2)}, u32[]{:S(2)}) collective-permute-start(bf16[256,1024]{0,1:T(8,128)(2,1)S(1)} %copy.106), channel_id=1, source_target_pairs={{28,0},{0,4},{4,8},{8,12},{12,16},{16,20},{20,24},{24,28},{29,1},{... | collective-permute-start | bytes 1572872 | tf_op jit(solution)/shard_map/while/body/eval_jaxpr/ppermute | solution.py:13
  451.2 50.0 %collective-permute-start.1 = (bf16[256,1024]{0,1:T(8,128)(2,1)}, bf16[256,1024]{0,1:T(8,128)(2,1)}, u32[]{:S(2)}, u32[]{:S(2)}) collective-permute-start(bf16[256,1024]{0,1:T(8,128)(2,1)} %copy.107), channel_id=1, source_target_pairs={{28,0},{0,4},{4,8},{8,12},{12,16},{16,20},{20,24},{24,28},{29,1},{... | collective-permute-start | bytes 1572872 | tf_op jit(solution)/shard_map/while/body/eval_jaxpr/ppermute | solution.py:13
  502.5 50.9 %collective-permute-start = (bf16[256,1024]{0,1:T(8,128)(2,1)S(1)}, bf16[256,1024]{0,1:T(8,128)(2,1)}, u32[]{:S(2)}, u32[]{:S(2)}) collective-permute-start(bf16[256,1024]{0,1:T(8,128)(2,1)S(1)} %copy.106), channel_id=1, source_target_pairs={{28,0},{0,4},{4,8},{8,12},{12,16},{16,20},{20,24},{24,28},{29,1},{... | collective-permute-start | bytes 1572872 | tf_op jit(solution)/shard_map/while/body/eval_jaxpr/ppermute | solution.py:13
  504.3 49.1 %collective-permute-start.1 = (bf16[256,1024]{0,1:T(8,128)(2,1)}, bf16[256,1024]{0,1:T(8,128)(2,1)}, u32[]{:S(2)}, u32[]{:S(2)}) collective-permute-start(bf16[256,1024]{0,1:T(8,128)(2,1)} %copy.107), channel_id=1, source_target_pairs={{28,0},{0,4},{4,8},{8,12},{12,16},{16,20},{20,24},{24,28},{29,1},{... | collective-permute-start | bytes 1572872 | tf_op jit(solution)/shard_map/while/body/eval_jaxpr/ppermute | solution.py:13
  554.7 50.0 %collective-permute-start = (bf16[256,1024]{0,1:T(8,128)(2,1)S(1)}, bf16[256,1024]{0,1:T(8,128)(2,1)}, u32[]{:S(2)}, u32[]{:S(2)}) collective-permute-start(bf16[256,1024]{0,1:T(8,128)(2,1)S(1)} %copy.106), channel_id=1, source_target_pairs={{28,0},{0,4},{4,8},{8,12},{12,16},{16,20},{20,24},{24,28},{29,1},{... | collective-permute-start | bytes 1572872 | tf_op jit(solution)/shard_map/while/body/eval_jaxpr/ppermute | solution.py:13
  556.6 48.1 %collective-permute-start.1 = (bf16[256,1024]{0,1:T(8,128)(2,1)}, bf16[256,1024]{0,1:T(8,128)(2,1)}, u32[]{:S(2)}, u32[]{:S(2)}) collective-permute-start(bf16[256,1024]{0,1:T(8,128)(2,1)} %copy.107), channel_id=1, source_target_pairs={{28,0},{0,4},{4,8},{8,12},{12,16},{16,20},{20,24},{24,28},{29,1},{... | collective-permute-start | bytes 1572872 | tf_op jit(solution)/shard_map/while/body/eval_jaxpr/ppermute | solution.py:13
  605.9 49.1 %collective-permute-start = (bf16[256,1024]{0,1:T(8,128)(2,1)S(1)}, bf16[256,1024]{0,1:T(8,128)(2,1)}, u32[]{:S(2)}, u32[]{:S(2)}) collective-permute-start(bf16[256,1024]{0,1:T(8,128)(2,1)S(1)} %copy.106), channel_id=1, source_target_pairs={{28,0},{0,4},{4,8},{8,12},{12,16},{16,20},{20,24},{24,28},{29,1},{... | collective-permute-start | bytes 1572872 | tf_op jit(solution)/shard_map/while/body/eval_jaxpr/ppermute | solution.py:13
  656.3 48.1 %collective-permute-start = (bf16[256,1024]{0,1:T(8,128)(2,1)S(1)}, bf16[256,1024]{0,1:T(8,128)(2,1)}, u32[]{:S(2)}, u32[]{:S(2)}) collective-permute-start(bf16[256,1024]{0,1:T(8,128)(2,1)S(1)} %copy.106), channel_id=1, source_target_pairs={{28,0},{0,4},{4,8},{8,12},{12,16},{16,20},{20,24},{24,28},{29,1},{... | collective-permute-start | bytes 1572872 | tf_op jit(solution)/shard_map/while/body/eval_jaxpr/ppermute | solution.py:13
  705.7 47.2 %collective-permute-start = (bf16[256,1024]{0,1:T(8,128)(2,1)S(1)}, bf16[256,1024]{0,1:T(8,128)(2,1)}, u32[]{:S(2)}, u32[]{:S(2)}) collective-permute-start(bf16[256,1024]{0,1:T(8,128)(2,1)S(1)} %copy.106), channel_id=1, source_target_pairs={{28,0},{0,4},{4,8},{8,12},{12,16},{16,20},{20,24},{24,28},{29,1},{... | collective-permute-start | bytes 1572872 | tf_op jit(solution)/shard_map/while/body/eval_jaxpr/ppermute | solution.py:13
  804.1 70.5 %reduce-scatter.9.cloned.1.call-start = ((), (), s32[]{:S(2)}) async-start(), calls=%async_computation.15 | async-start | bytes 2621440 | tf_op jit(solution)/shard_map/reduce_scatter | solution.py:108
  806.3 95.2 %reduce-scatter.11.cloned.1.call-start = ((), (), s32[]{:S(2)}) async-start(), calls=%async_computation.16 | async-start | bytes 2621440 | tf_op jit(solution)/shard_map/reduce_scatter | solution.py:108
  808.4 127.1 %reduce-scatter.13.cloned.1.call-start = ((), (), s32[]{:S(2)}) async-start(), calls=%async_computation.17 | async-start | bytes 2621440 | tf_op jit(solution)/shard_map/reduce_scatter | solution.py:108
  812.2 197.6 %reduce-scatter.15.cloned.1.call-start = ((), (), s32[]{:S(2)}) async-start(), calls=%async_computation.18 | async-start | bytes 10485760 | tf_op jit(solution)/shard_map/reduce_scatter | solution.py:108
  819.6 264.6 %reduce-scatter.17.cloned.1.call-start = ((), (), s32[]{:S(2)}) async-start(), calls=%async_computation.19 | async-start | bytes 10485760 | tf_op jit(solution)/shard_map/reduce_scatter | solution.py:108
  (106 other events, 1996.0 us)
Sparse Core Ops, SparseCore 0:
  9.6 25.2 all-gather.8
  36.5 22.5 all-gather.14
  60.7 22.5 all-gather.12
  85.8 73.3 all-gather.10
  161.8 71.6 all-gather.16
  234.9 20.8 all-gather.18
  257.4 58.2 all-gather.20
  317.3 58.2 all-gather.22
  804.2 28.1 reduce-scatter.6
  834.9 32.4 reduce-scatter.8
  870.0 31.4 reduce-scatter.10
  904.0 31.4 reduce-scatter.12
  938.1 71.6 reduce-scatter.14
  1012.4 71.6 reduce-scatter.16
where the time goes:
time: 1590 us; the launch traced here: 1580 us
  waiting for transfers between devices  689 us (43%)
  blocking collectives  524 us (33%)
  matrix products  194 us (12%)
  other arithmetic  85.1 us (5%)
  local copies, waits for them, and re-layouts  59 us (4%)
    psum x1, blocking collectives, body(): lax.psum((share_query, share_key, share_value, share_out, share_up, share...  485 us
    ppermute x32, waiting for transfers between devices, from_behind(): return lax.ppermute(block, axis, route)  247 us
    reduce_scatter x6, waiting for transfers between devices, owner_rows(): lax.psum_scatter(lax.dot_general(layer_in, layer_grad, (((0,), (0,)), (()...  210 us
    all_gather x1, waiting for transfers between devices, body(): value_piece = lax.all_gather(values, 'ctx', axis=0, tiled=True)  74.2 us
    all_gather x1, waiting for transfers between devices, body(): key_piece = lax.all_gather(key_rows, 'ctx', axis=0, tiled=True)  73.5 us
    psum x1, blocking collectives, body(): lax.psum((grad_query_b, grad_value_b, grad_output_b, grad_attn_gain, grad...  38.5 us
    dot_general x8, matrix products, online_update(): jnp.einsum('hqk,khd->qhd', exp_scores.astype(jnp.bfloat16), value_rows.re...  37.9 us
    while x120, local copies, waits for them, and re-layouts  34.6 us
  transfers between devices with their start and end apart: 46, of which 26 were waited for; matrix products, arithmetic and copies ran while one was open for 18% of the time, Pallas kernels for 0%

commit v1 on v0

--- a/solution.py
+++ b/solution.py
@@ -177,8 +177,11 @@
         jnp.full((H, block_len), -1e30, jnp.float32),
         jnp.zeros((H, block_len), jnp.float32),
     )
-    key_piece = lax.all_gather(key_rows, "ctx", axis=0, tiled=True)
-    value_piece = lax.all_gather(values, "ctx", axis=0, tiled=True)
+    key_piece, value_piece = jnp.split(
+        lax.all_gather(jnp.concatenate([key_rows, values], axis=1), "ctx", axis=0, tiled=True),
+        [key_rows.shape[1]],
+        axis=1,
+    )
     shards = key_piece.shape[0] // block_len
 
     def one_shard(index, inner):

time: 1590 us -> 1530 us (0.962)
  waiting for transfers between devices: 689 us -> 630 us
    reduce_scatter x6, waiting for transfers between devices: 210 us -> 178 us  [owner_rows(): lax.psum_scatter(lax.dot_general(layer_in, layer_grad, (((0,), (0,)), (()...]
    all_gather x2 -> x1, waiting for transfers between devices: 148 us -> 125 us  [body(): lax.all_gather(jnp.concatenate([key_rows, values], axis=1), 'ctx', axis=0...]
  transfers between devices with their start and end apart: 46 -> 45, of which waited for: 26 -> 24; matrix products, arithmetic and copies ran while one was open for 18% -> 20% of each run, Pallas kernels for 0% -> 0%
where the time goes in v1:
time: 1530 us
  waiting for transfers between devices  630 us (41%)
  blocking collectives  524 us (34%)
  matrix products  194 us (13%)
  other arithmetic  84.6 us (6%)
  local copies, waits for them, and re-layouts  66 us (4%)
    psum x1, blocking collectives, body(): lax.psum((share_query, share_key, share_value, share_out, share_up, share...  485 us
    ppermute x32, waiting for transfers between devices, from_behind(): return lax.ppermute(block, axis, route)  247 us
    reduce_scatter x6, waiting for transfers between devices, owner_rows(): lax.psum_scatter(lax.dot_general(layer_in, layer_grad, (((0,), (0,)), (()...  178 us
    all_gather x1, waiting for transfers between devices, body(): lax.all_gather(jnp.concatenate([key_rows, values], axis=1), 'ctx', axis=0...  125 us
    psum x1, blocking collectives, body(): lax.psum((grad_query_b, grad_value_b, grad_output_b, grad_attn_gain, grad...  38.7 us
    dot_general x8, matrix products, online_update(): jnp.einsum('hqk,khd->qhd', exp_scores.astype(jnp.bfloat16), value_rows.re...  37.5 us
    while x120, local copies, waits for them, and re-layouts  34.6 us
    dot_general x6, matrix products, dense(): return jnp.dot(left, right, preferred_element_type=jnp.float32)  32.1 us
  transfers between devices with their start and end apart: 45, of which 24 were waited for; matrix products, arithmetic and copies ran while one was open for 20% of the time, Pallas kernels for 0%

profile of v1, /device:TPU:0, one launch (start us, length us, event | category | flops | bytes accessed | tf_op | source)
XLA Modules:
  0.0 1527.5 jit_solution(17174053871141192915)
XLA Ops:
  9.5 25.4 %all-gather.8.cloned.1.call-done = bf16[1024,1024]{1,0:T(8,128)(2,1)} async-done(((bf16[256,1024]{1,0:T(8,128)(2,1)}), bf16[1024,1024]{1,0:T(8,128)(2,1)}) %all-gather.8.cloned.1.call-update) | async-done | bytes 2097168 | tf_op jit(solution)/shard_map/all_gather | solution.py:165
  37.4 21.7 %all-gather.10.cloned.1.call-done = bf16[1024,1024]{1,0:T(8,128)(2,1)} async-done(((bf16[256,1024]{1,0:T(8,128)(2,1)}), bf16[1024,1024]{1,0:T(8,128)(2,1)}) %all-gather.10.cloned.1.call-update) | async-done | bytes 2097168 | tf_op jit(solution)/shard_map/all_gather | solution.py:166
  68.1 15.2 all-gather.14.cloned.1.call-done
  85.8 125.0 %all-gather.12.cloned.1.call-done = bf16[2048,2048]{1,0:T(8,128)(2,1)} async-done(((bf16[256,2048]{1,0:T(8,128)(2,1)}), bf16[2048,2048]{1,0:T(8,128)(2,1)}) %all-gather.12.cloned.1.call-update) | async-done | bytes 8388624 | tf_op jit(solution)/shard_map/all_gather | solution.py:181
  217.1 101.5 %while.42 = (s32[]{:T(128)}, f32[256,16,64]{0,2,1:T(8,128)}, f32[16,256]{1,0:T(8,128)S(1)}, f32[16,256]{1,0:T(8,128)S(1)}, s32[256]{0:T(256)S(1)}, /*index=5*/s3...) while((s32[]{:T(128)}, f32[256,16,64]{0,2,1:T(8,128)}, ...), condition=%wide.region_6.7_spmd.clone, body=%wide.region_3.6_spmd.clone.sunk | while | flops 282943488 | bytes 20975804 | solution.py:193
  322.8 15.9 %fusion.29 = (bf16[256,4096]{1,0:T(8,128)(2,1)}, f32[256,4096]{1,0:T(8,128)}) fusion(f32[4096]{0:T(1024)S(1)} %copy-done.28, bf16[1024,4096]{1,0:T(8,128)(2,1)} %all-gather.18.cloned.1.call-done, f32[256,1024]{1,0:T(8,128)S(1)} %get-tuple-element.760, f32[1024]{0:T(1024)S(1)} %copy-done.23, f32[1024]{0:T(1024)S(1)} %copy-done.22, ...), kind=kOutput, calls=%fused_computation.46 | convolution fusion | flops 2218000384 | bytes 15755264 | tf_op jit(solution)/shard_map/dot_general | solution.py:17
  338.8 13.9 all-gather.20.cloned.1.call-done
  375.6 406.6 %while.43 = (s32[]{:T(128)}, bf16[256,1024]{0,1:T(8,128)(2,1)}, bf16[256,1024]{0,1:T(8,128)(2,1)}, f32[256,1024]{0,1:T(8,128)}, f32[256,1024]{0,1:T(8,128)}, /*i...) while((s32[]{:T(128)}, bf16[256,1024]{0,1:T(8,128)(2,1)}, ...), condition=%wide.region_16.17_spmd.clone, body=%wide.region_15.16_spmd.clone.sunk | while | flops 686882816 | bytes 68932264 | solution.py:240
  395.8 21.2 %collective-permute-done.2 = bf16[256,1024]{0,1:T(8,128)(2,1)} collective-permute-done((bf16[256,1024]{0,1:T(8,128)(2,1)}, bf16[256,1024]{0,1:T(8,128)(2,1)}, u32[]{:S(2)}, u32[]{:S(2)}) %collective-permute-start.2) | collective-permute-done | bytes 524320 | tf_op jit(solution)/shard_map/while/body/eval_jaxpr/ppermute | solution.py:13
  419.1 8.5 collective-permute-done.3
  447.8 23.2 %collective-permute-done.2 = bf16[256,1024]{0,1:T(8,128)(2,1)} collective-permute-done((bf16[256,1024]{0,1:T(8,128)(2,1)}, bf16[256,1024]{0,1:T(8,128)(2,1)}, u32[]{:S(2)}, u32[]{:S(2)}) %collective-permute-start.2) | collective-permute-done | bytes 524320 | tf_op jit(solution)/shard_map/while/body/eval_jaxpr/ppermute | solution.py:13
  473.2 7.6 collective-permute-done.3
  499.2 25.0 %collective-permute-done.2 = bf16[256,1024]{0,1:T(8,128)(2,1)} collective-permute-done((bf16[256,1024]{0,1:T(8,128)(2,1)}, bf16[256,1024]{0,1:T(8,128)(2,1)}, u32[]{:S(2)}, u32[]{:S(2)}) %collective-permute-start.2) | collective-permute-done | bytes 524320 | tf_op jit(solution)/shard_map/while/body/eval_jaxpr/ppermute | solution.py:13
  549.6 26.8 %collective-permute-done.2 = bf16[256,1024]{0,1:T(8,128)(2,1)} collective-permute-done((bf16[256,1024]{0,1:T(8,128)(2,1)}, bf16[256,1024]{0,1:T(8,128)(2,1)}, u32[]{:S(2)}, u32[]{:S(2)}) %collective-permute-start.2) | collective-permute-done | bytes 524320 | tf_op jit(solution)/shard_map/while/body/eval_jaxpr/ppermute | solution.py:13
  600.5 27.2 %collective-permute-done.2 = bf16[256,1024]{0,1:T(8,128)(2,1)} collective-permute-done((bf16[256,1024]{0,1:T(8,128)(2,1)}, bf16[256,1024]{0,1:T(8,128)(2,1)}, u32[]{:S(2)}, u32[]{:S(2)}) %collective-permute-start.2) | collective-permute-done | bytes 524320 | tf_op jit(solution)/shard_map/while/body/eval_jaxpr/ppermute | solution.py:13
  650.8 27.2 %collective-permute-done.2 = bf16[256,1024]{0,1:T(8,128)(2,1)} collective-permute-done((bf16[256,1024]{0,1:T(8,128)(2,1)}, bf16[256,1024]{0,1:T(8,128)(2,1)}, u32[]{:S(2)}, u32[]{:S(2)}) %collective-permute-start.2) | collective-permute-done | bytes 524320 | tf_op jit(solution)/shard_map/while/body/eval_jaxpr/ppermute | solution.py:13
  700.3 26.6 %collective-permute-done.2 = bf16[256,1024]{0,1:T(8,128)(2,1)} collective-permute-done((bf16[256,1024]{0,1:T(8,128)(2,1)}, bf16[256,1024]{0,1:T(8,128)(2,1)}, u32[]{:S(2)}, u32[]{:S(2)}) %collective-permute-start.2) | collective-permute-done | bytes 524320 | tf_op jit(solution)/shard_map/while/body/eval_jaxpr/ppermute | solution.py:13
  748.8 25.7 %collective-permute-done.2 = bf16[256,1024]{0,1:T(8,128)(2,1)} collective-permute-done((bf16[256,1024]{0,1:T(8,128)(2,1)}, bf16[256,1024]{0,1:T(8,128)(2,1)}, u32[]{:S(2)}, u32[]{:S(2)}) %collective-permute-start.2) | collective-permute-done | bytes 524320 | tf_op jit(solution)/shard_map/while/body/eval_jaxpr/ppermute | solution.py:13
  791.2 7.4 convolution_convert_fusion.1
  808.6 38.7 %all-reduce = (f32[1024]{0:T(1024)}, f32[1024]{0:T(1024)}, f32[1024]{0:T(1024)}, f32[1024]{0:T(1024)}, f32[1024]{0:T(1024)}, /*index=5*/f32[4096]{0:T(1024)}, f32[1024]{0:T(1024)}, f32[1024]{0:T(1024)}, f32[1024]{0:T(1024)}) all-reduce(f32[1024]{0:T(1024)S(1)} %convert_reduce_fusion.5, ...), channel_id=1, replica_groups=mesh['ctx'=8,'fsdp'=4] {'ctx','fsdp'}, use_global_device_ids=true, to_apply=%region_20.21 | all-reduce | flops 12288 | bytes 98304 | tf_op jit(solution)/shard_map/psum | solution.py:269
  854.0 29.0 %reduce-scatter.11.cloned.1.call-done = bf16[256,1024]{0,1:T(8,128)(2,1)} async-done(((bf16[1024,1024]{0,1:T(8,128)(2,1)}), bf16[256,1024]{0,1:T(8,128)(2,1)}) %reduce-scatter.11.cloned.1.call-update) | async-done | bytes 524304 | tf_op jit(solution)/shard_map/reduce_scatter | solution.py:108
  883.0 74.2 %reduce-scatter.15.cloned.1.call-done = bf16[256,4096]{1,0:T(8,128)(2,1)} async-done(((bf16[1024,4096]{1,0:T(8,128)(2,1)}), bf16[256,4096]{1,0:T(8,128)(2,1)}) %reduce-scatter.15.cloned.1.call-update) | async-done | bytes 2097168 | tf_op jit(solution)/shard_map/reduce_scatter | solution.py:108
  957.2 74.5 %reduce-scatter.17.cloned.1.call-done = bf16[1024,1024]{1,0:T(8,128)(2,1)} async-done(((bf16[4096,1024]{1,0:T(8,128)(2,1)}), bf16[1024,1024]{1,0:T(8,128)(2,1)}) %reduce-scatter.17.cloned.1.call-update) | async-done | bytes 2097168 | tf_op jit(solution)/shard_map/reduce_scatter | solution.py:108
  1031.7 485.2 %all-reduce.3 = (f32[256,1024]{0,1:T(8,128)S(1)}, f32[256,1024]{0,1:T(8,128)S(1)}, f32[256,1024]{0,1:T(8,128)S(1)}, f32[256,1024]{1,0:T(8,128)}, f32[256,4096]{1,0:T(8,128)}, /*index=5*/f32[1024,1024]{1,0:T(8,128)}) all-reduce(bf16[256,1024]{0,1:T(8,128)(2,1)} %reduce-scatter.7.cloned.1.call-done, ...), channel_id=1, replica_groups=mesh['ctx'=8,'fsdp'=4] {'ctx'}, use_global_device_ids=true, to_apply=%region_18.19 | all-reduce | flops 3145728 | bytes 18874368 | tf_op jit(solution)/shard_map/psum | solution.py:256
  (504 shorter events, 366.2 us)
Async XLA Ops:
  7.9 51.2 %all-gather.10.cloned.1.call-start = ((), (), s32[]{:S(2)}) async-start(), calls=%async_computation.7 | async-start | bytes 2621440 | tf_op jit(solution)/shard_map/all_gather | solution.py:166
  8.7 74.6 %all-gather.14.cloned.1.call-start = ((), (), s32[]{:S(2)}) async-start(), calls=%async_computation.9 | async-start | bytes 2621440 | tf_op jit(solution)/shard_map/all_gather | solution.py:164
  9.4 201.4 %all-gather.12.cloned.1.call-start = ((), (), s32[]{:S(2)}) async-start(), calls=%async_computation.8 | async-start | bytes 9437184 | tf_op jit(solution)/shard_map/all_gather | solution.py:181
  62.5 257.5 %all-gather.16.cloned.1.call-start = ((), (), s32[]{:S(2)}) async-start(), calls=%async_computation.10 | async-start | bytes 2621440 | tf_op jit(solution)/shard_map/all_gather | solution.py:167
  63.1 259.6 %all-gather.18.cloned.1.call-start = ((), (), s32[]{:S(2)}) async-start(), calls=%async_computation.11 | async-start | bytes 10485760 | tf_op jit(solution)/shard_map/all_gather | solution.py:168
  63.7 288.9 %all-gather.20.cloned.1.call-start = ((), (), s32[]{:S(2)}) async-start(), calls=%async_computation.12 | async-start | bytes 10485760 | tf_op jit(solution)/shard_map/all_gather | solution.py:169
  64.5 789.6 %reduce-scatter.13.cloned.1.call-start = ((), (), s32[]{:S(2)}) async-start(), calls=%async_computation.16 | async-start | bytes 2621440 | tf_op jit(solution)/shard_map/reduce_scatter | solution.py:108
  375.5 478.5 %reduce-scatter.7.cloned.1.call-start = ((), (), s32[]{:S(2)}) async-start(), calls=%async_computation.13 | async-start | bytes 2621440 | tf_op jit(solution)/shard_map/reduce_scatter | solution.py:108
  377.0 52.7 %collective-permute-start = (bf16[256,1024]{0,1:T(8,128)(2,1)S(1)}, bf16[256,1024]{0,1:T(8,128)(2,1)}, u32[]{:S(2)}, u32[]{:S(2)}) collective-permute-start(bf16[256,1024]{0,1:T(8,128)(2,1)S(1)} %copy.106), channel_id=1, source_target_pairs={{28,0},{0,4},{4,8},{8,12},{12,16},{16,20},{20,24},{24,28},{29,1},{... | collective-permute-start | bytes 1572872 | tf_op jit(solution)/shard_map/while/body/eval_jaxpr/ppermute | solution.py:13
  380.3 49.4 %collective-permute-start.1 = (bf16[256,1024]{0,1:T(8,128)(2,1)}, bf16[256,1024]{0,1:T(8,128)(2,1)}, u32[]{:S(2)}, u32[]{:S(2)}) collective-permute-start(bf16[256,1024]{0,1:T(8,128)(2,1)} %copy.107), channel_id=1, source_target_pairs={{28,0},{0,4},{4,8},{8,12},{12,16},{16,20},{20,24},{24,28},{29,1},{... | collective-permute-start | bytes 1572872 | tf_op jit(solution)/shard_map/while/body/eval_jaxpr/ppermute | solution.py:13
  430.9 51.9 %collective-permute-start = (bf16[256,1024]{0,1:T(8,128)(2,1)S(1)}, bf16[256,1024]{0,1:T(8,128)(2,1)}, u32[]{:S(2)}, u32[]{:S(2)}) collective-permute-start(bf16[256,1024]{0,1:T(8,128)(2,1)S(1)} %copy.106), channel_id=1, source_target_pairs={{28,0},{0,4},{4,8},{8,12},{12,16},{16,20},{20,24},{24,28},{29,1},{... | collective-permute-start | bytes 1572872 | tf_op jit(solution)/shard_map/while/body/eval_jaxpr/ppermute | solution.py:13
  432.8 50.0 %collective-permute-start.1 = (bf16[256,1024]{0,1:T(8,128)(2,1)}, bf16[256,1024]{0,1:T(8,128)(2,1)}, u32[]{:S(2)}, u32[]{:S(2)}) collective-permute-start(bf16[256,1024]{0,1:T(8,128)(2,1)} %copy.107), channel_id=1, source_target_pairs={{28,0},{0,4},{4,8},{8,12},{12,16},{16,20},{20,24},{24,28},{29,1},{... | collective-permute-start | bytes 1572872 | tf_op jit(solution)/shard_map/while/body/eval_jaxpr/ppermute | solution.py:13
  484.1 50.9 %collective-permute-start = (bf16[256,1024]{0,1:T(8,128)(2,1)S(1)}, bf16[256,1024]{0,1:T(8,128)(2,1)}, u32[]{:S(2)}, u32[]{:S(2)}) collective-permute-start(bf16[256,1024]{0,1:T(8,128)(2,1)S(1)} %copy.106), channel_id=1, source_target_pairs={{28,0},{0,4},{4,8},{8,12},{12,16},{16,20},{20,24},{24,28},{29,1},{... | collective-permute-start | bytes 1572872 | tf_op jit(solution)/shard_map/while/body/eval_jaxpr/ppermute | solution.py:13
  486.0 49.1 %collective-permute-start.1 = (bf16[256,1024]{0,1:T(8,128)(2,1)}, bf16[256,1024]{0,1:T(8,128)(2,1)}, u32[]{:S(2)}, u32[]{:S(2)}) collective-permute-start(bf16[256,1024]{0,1:T(8,128)(2,1)} %copy.107), channel_id=1, source_target_pairs={{28,0},{0,4},{4,8},{8,12},{12,16},{16,20},{20,24},{24,28},{29,1},{... | collective-permute-start | bytes 1572872 | tf_op jit(solution)/shard_map/while/body/eval_jaxpr/ppermute | solution.py:13
  536.3 50.0 %collective-permute-start = (bf16[256,1024]{0,1:T(8,128)(2,1)S(1)}, bf16[256,1024]{0,1:T(8,128)(2,1)}, u32[]{:S(2)}, u32[]{:S(2)}) collective-permute-start(bf16[256,1024]{0,1:T(8,128)(2,1)S(1)} %copy.106), channel_id=1, source_target_pairs={{28,0},{0,4},{4,8},{8,12},{12,16},{16,20},{20,24},{24,28},{29,1},{... | collective-permute-start | bytes 1572872 | tf_op jit(solution)/shard_map/while/body/eval_jaxpr/ppermute | solution.py:13
  538.2 48.1 %collective-permute-start.1 = (bf16[256,1024]{0,1:T(8,128)(2,1)}, bf16[256,1024]{0,1:T(8,128)(2,1)}, u32[]{:S(2)}, u32[]{:S(2)}) collective-permute-start(bf16[256,1024]{0,1:T(8,128)(2,1)} %copy.107), channel_id=1, source_target_pairs={{28,0},{0,4},{4,8},{8,12},{12,16},{16,20},{20,24},{24,28},{29,1},{... | collective-permute-start | bytes 1572872 | tf_op jit(solution)/shard_map/while/body/eval_jaxpr/ppermute | solution.py:13
  587.6 49.1 %collective-permute-start = (bf16[256,1024]{0,1:T(8,128)(2,1)S(1)}, bf16[256,1024]{0,1:T(8,128)(2,1)}, u32[]{:S(2)}, u32[]{:S(2)}) collective-permute-start(bf16[256,1024]{0,1:T(8,128)(2,1)S(1)} %copy.106), channel_id=1, source_target_pairs={{28,0},{0,4},{4,8},{8,12},{12,16},{16,20},{20,24},{24,28},{29,1},{... | collective-permute-start | bytes 1572872 | tf_op jit(solution)/shard_map/while/body/eval_jaxpr/ppermute | solution.py:13
  589.4 47.2 %collective-permute-start.1 = (bf16[256,1024]{0,1:T(8,128)(2,1)}, bf16[256,1024]{0,1:T(8,128)(2,1)}, u32[]{:S(2)}, u32[]{:S(2)}) collective-permute-start(bf16[256,1024]{0,1:T(8,128)(2,1)} %copy.107), channel_id=1, source_target_pairs={{28,0},{0,4},{4,8},{8,12},{12,16},{16,20},{20,24},{24,28},{29,1},{... | collective-permute-start | bytes 1572872 | tf_op jit(solution)/shard_map/while/body/eval_jaxpr/ppermute | solution.py:13
  637.9 48.1 %collective-permute-start = (bf16[256,1024]{0,1:T(8,128)(2,1)S(1)}, bf16[256,1024]{0,1:T(8,128)(2,1)}, u32[]{:S(2)}, u32[]{:S(2)}) collective-permute-start(bf16[256,1024]{0,1:T(8,128)(2,1)S(1)} %copy.106), channel_id=1, source_target_pairs={{28,0},{0,4},{4,8},{8,12},{12,16},{16,20},{20,24},{24,28},{29,1},{... | collective-permute-start | bytes 1572872 | tf_op jit(solution)/shard_map/while/body/eval_jaxpr/ppermute | solution.py:13
  687.3 47.2 %collective-permute-start = (bf16[256,1024]{0,1:T(8,128)(2,1)S(1)}, bf16[256,1024]{0,1:T(8,128)(2,1)}, u32[]{:S(2)}, u32[]{:S(2)}) collective-permute-start(bf16[256,1024]{0,1:T(8,128)(2,1)S(1)} %copy.106), channel_id=1, source_target_pairs={{28,0},{0,4},{4,8},{8,12},{12,16},{16,20},{20,24},{24,28},{29,1},{... | collective-permute-start | bytes 1572872 | tf_op jit(solution)/shard_map/while/body/eval_jaxpr/ppermute | solution.py:13
  785.7 68.3 %reduce-scatter.9.cloned.1.call-start = ((), (), s32[]{:S(2)}) async-start(), calls=%async_computation.14 | async-start | bytes 2621440 | tf_op jit(solution)/shard_map/reduce_scatter | solution.py:108
  787.9 95.1 %reduce-scatter.11.cloned.1.call-start = ((), (), s32[]{:S(2)}) async-start(), calls=%async_computation.15 | async-start | bytes 2621440 | tf_op jit(solution)/shard_map/reduce_scatter | solution.py:108
  791.1 166.1 %reduce-scatter.15.cloned.1.call-start = ((), (), s32[]{:S(2)}) async-start(), calls=%async_computation.17 | async-start | bytes 10485760 | tf_op jit(solution)/shard_map/reduce_scatter | solution.py:108
  798.6 233.1 %reduce-scatter.17.cloned.1.call-start = ((), (), s32[]{:S(2)}) async-start(), calls=%async_computation.18 | async-start | bytes 10485760 | tf_op jit(solution)/shard_map/reduce_scatter | solution.py:108
  (102 other events, 1805.3 us)
Sparse Core Ops, SparseCore 0:
  9.6 25.2 all-gather.7
  36.5 22.5 all-gather.9
  60.7 22.5 all-gather.13
  85.8 124.9 all-gather.11
  212.2 20.7 all-gather.15
  234.4 58.2 all-gather.17
  294.3 58.2 all-gather.19
  375.6 31.4 reduce-scatter.12
  785.9 27.9 reduce-scatter.6
  816.2 32.5 reduce-scatter.8
  851.5 31.4 reduce-scatter.10
  885.4 71.6 reduce-scatter.14
  959.9 71.6 reduce-scatter.16
